TPU v7x, 32 devices: a whole 2x2x4 slice. The times are simulated.
32 devices in a mesh: img: 4 (over y, core), ref: 8 (over z, x).
Axes of the slice: x: 2, y: 2, z: 4, core: 2. Of those that a mesh axis runs over, the one named last changes fastest.
Arguments:
- images: float32 [2, 64, 32768], P(None, 'img', 'ref'), may hold values from -6 to 6
- references: float32 [2, 64, 32768], P(None, 'ref', 'img'), may hold values from -2 to 2
- precision: float32 [64], P('img'), may hold values from 0.00390625 to 0.0390625
- shifts: int32 [12, 2], replicated, may hold values from -6 to 6, as said below
- labels: int32 [64], P('ref'), may hold values from 0 to 3
- log_prior: float32 [4], replicated, may hold values from -4 to 4
Outputs:
- new_refs: float32 [2, 64, 32768], P(None, 'ref', 'img')
- class_post: float32 [64, 4], P('img')
Inputs may be any that keep to these rules, and one draw needn't show every extreme that they name: `shifts`: both ends of the range occur in every draw.
All inputs are finite; a program needn't handle non-finite values.
Results may differ from a plain program's by a relative error of at most 0.0056.
Values may be sent and summed in bfloat16 or wider, within the bound.
A program may use at most 64 MiB of HBM per device.

v0:
```python
import math

import jax
import jax.numpy as jnp
from jax import lax
from jax.sharding import PartitionSpec as P

ROWS = 256
COLS = 128
SHIFTS = 12
CLASSES = 4


def phases(shifts):
    index = jnp.arange(ROWS * COLS, dtype=jnp.int32)
    freq_y = (index // COLS - ROWS // 2).astype(jnp.float32)
    freq_x = (index % COLS).astype(jnp.float32)
    shift_x = shifts[:, 0].astype(jnp.float32)[:, None]
    shift_y = shifts[:, 1].astype(jnp.float32)[:, None]
    angles = 2.0 * math.pi / ROWS * (freq_x[None, :] * shift_x + freq_y[None, :] * shift_y)
    return (jnp.cos(angles), jnp.sin(angles))


def inner_rows(left, right):
    return lax.dot_general(
        left, right, (((1,), (1,)), ((), ())), preferred_element_type=jnp.float32
    )


def inner_cols(left, right):
    return lax.dot_general(
        left, right, (((0,), (0,)), ((), ())), preferred_element_type=jnp.float32
    )


def local(images, references, precision, shifts, labels, log_prior):
    img_low = lax.all_gather(images.astype(jnp.bfloat16), "ref", axis=2, tiled=True)
    ref_low = lax.all_gather(references.astype(jnp.bfloat16), "img", axis=2, tiled=True)
    pixels = img_low.shape[2]
    img_dev = img_low.shape[1]
    ref_dev = ref_low.shape[1]
    blocks = SHIFTS // 4
    cosine, sine_part = phases(shifts)
    cos_blocks = cosine.reshape(blocks, 4, pixels)
    sin_blocks = sine_part.reshape(blocks, 4, pixels)
    ref_wide = ref_low.astype(jnp.float32)
    energy = jnp.sum(ref_wide * ref_wide, axis=(0, 2))
    onehot = (labels[:, None] == jnp.arange(CLASSES, dtype=jnp.int32)[None, :]).astype(jnp.float32)
    prior_term = jnp.sum(onehot * log_prior[None, :], axis=1)

    def cross_block(operands):
        cos_rows, sin_rows = operands
        shifted_re = (
            ref_wide[0][None] * cos_rows[:, None, :] + ref_wide[1][None] * sin_rows[:, None, :]
        ).astype(jnp.bfloat16)
        shifted_im = (
            ref_wide[1][None] * cos_rows[:, None, :] - ref_wide[0][None] * sin_rows[:, None, :]
        ).astype(jnp.bfloat16)
        return inner_rows(img_low[0], shifted_re.reshape(4 * ref_dev, pixels)) + inner_rows(
            img_low[1], shifted_im.reshape(4 * ref_dev, pixels)
        )

    cross_terms = lax.map(cross_block, (cos_blocks, sin_blocks))
    cross_terms = jnp.transpose(cross_terms, (1, 0, 2)).reshape(img_dev, SHIFTS, ref_dev)
    scores = (
        precision[:, None, None] * (cross_terms - 0.5 * energy[None, None, :])
        + prior_term[None, None, :]
    )
    local_top = jnp.max(scores, axis=(1, 2))
    top_score = lax.pmax(local_top, "ref")
    exponent = jnp.exp(scores - top_score[:, None, None])
    local_class = jnp.einsum(
        "ik,kc->ic", jnp.sum(exponent, axis=1), onehot, precision=lax.Precision.HIGHEST
    )
    row_total, class_sum = lax.psum((jnp.sum(exponent, axis=(1, 2)), local_class), "ref")
    posterior = exponent / row_total[:, None, None]
    class_post = class_sum / row_total[:, None]
    local_mass = jnp.sum(posterior, axis=(0, 1))
    post_low = posterior.astype(jnp.bfloat16).reshape(img_dev, blocks, 4 * ref_dev)
    post_low = jnp.transpose(post_low, (1, 0, 2))

    def back_block(running, operands):
        weights_blk, cos_rows, sin_rows = operands
        back_re = inner_cols(weights_blk, img_low[0]).reshape(4, ref_dev, pixels)
        back_im = inner_cols(weights_blk, img_low[1]).reshape(4, ref_dev, pixels)
        part_re = jnp.sum(back_re * cos_rows[:, None, :] - back_im * sin_rows[:, None, :], axis=0)
        part_im = jnp.sum(back_im * cos_rows[:, None, :] + back_re * sin_rows[:, None, :], axis=0)
        return (running + jnp.stack([part_re, part_im]), None)

    start_sum = jnp.zeros((2, ref_dev, pixels), jnp.float32)
    summed, unused = lax.scan(back_block, start_sum, (post_low, cos_blocks, sin_blocks))
    summed_part = lax.psum_scatter(summed, "img", scatter_dimension=2, tiled=True)
    ref_mass = lax.psum(local_mass, "img")
    new_refs = summed_part / (ref_mass + 1.0)[None, :, None]
    return (new_refs, class_post)


def solution(mesh):
    return jax.shard_map(
        local,
        mesh=mesh,
        in_specs=(P(None, "img", "ref"), P(None, "ref", "img"), P("img"), P(), P("ref"), P()),
        out_specs=(P(None, "ref", "img"), P("img", None)),
        check_vma=False,
    )
```

profile of v0, /device:TPU:25, one launch (start us, length us, event | category | flops | bytes accessed | tf_op | source)
XLA Modules:
  0.0 194.5 jit_solution(2304866552472069872)
XLA Ops:
  7.2 1.8 convert_element_type.63
  9.1 1.8 convert_element_type.69
  11.2 12.6 %fusion.39 = (f32[3,4,32768]{2,1,0:T(4,128)}, f32[3,4,32768]{2,1,0:T(4,128)}) fusion(f32[3,4]{1,0:T(4,128)S(1)} %mul.204, f32[32768]{0:T(1024)S(1)} %get-tuple-element.128, f32[3,4]{1,0:T(4,128)S(1)} %mul.200, f32[32768]{0:T(1024)S(1)} %get-tuple-element.127), kind=kLoop, calls=%fused_computation.44 | loop fusion | flops 1572864 | bytes 3407968 | tf_op jit(solution)/shard_map/sin | solution.py:21
  24.0 4.3 %all-gather.3.cloned.1.call-done = bf16[2,8,32768]{2,1,0:T(8,128)(2,1)} async-done(((bf16[2,8,8192]{2,1,0:T(8,128)(2,1)}), bf16[2,8,32768]{2,1,0:T(8,128)(2,1)}) %all-gather.3.cloned.1.call-update) | async-done | bytes 1048592 | tf_op jit(solution)/shard_map/all_gather | solution.py:38
  28.3 1.9 multiply_reduce_fusion
  30.3 1.4 convert_element_type.64
  31.6 46.2 %all-gather.5.cloned.1.call-done = bf16[2,16,32768]{2,1,0:T(8,128)(2,1)} async-done(((bf16[2,16,4096]{2,1,0:T(8,128)(2,1)}), bf16[2,16,32768]{2,1,0:T(8,128)(2,1)}) %all-gather.5.cloned.1.call-update) | async-done | bytes 2097168 | tf_op jit(solution)/shard_map/all_gather | solution.py:37
  77.8 12.7 %while.21 = (s32[]{:T(128)}, f32[3,16,32]{2,1,0:T(8,128)S(1)}, f32[2,8,32768]{2,1,0:T(8,128)S(1)}, f32[3,4,32768]{2,1,0:T(4,128)}, f32[3,4,32768]{2,1,0:T(4,128)}, /*index=5*/bf16[2,16,32768]{2,1,0:T(8,128)(2,1)}, s32[]{:T(128)}) while((s32[]{:T(128)}, f32[3,16,32]{2,1,0:T(8,128)S(1)}, f32[2,8,32768]{2,1,0:T(8,128)S(1)}, ...), condition=%wide.region_1.2_spmd, body=%wide.region_0.1_spmd.sunk | while | flops 75497984 | bytes 23087216 | solution.py:63
  77.8 1.3 dynamic-slice_bitcast_fusion.6
  79.1 0.1 slice_bitcast_fusion.3
  79.3 1.4 copy-done.1
  80.7 0.7 fusion.69
  81.4 0.7 fusion.70
  82.1 1.3 dynamic-slice_bitcast_fusion.6
  83.4 0.1 slice_bitcast_fusion.3
  83.5 1.4 copy-done.1
  84.9 0.7 fusion.69
  85.6 0.7 fusion.70
  86.3 1.3 dynamic-slice_bitcast_fusion.6
  87.6 0.1 slice_bitcast_fusion.3
  87.8 1.4 copy-done.1
  89.2 0.7 fusion.69
  89.9 0.7 fusion.70
  90.8 12.1 %pmax.7 = f32[16]{0:T(128)S(1)} all-reduce(f32[16]{0:T(128)S(1)} %fusion.52), channel_id=1, replica_groups=mesh['img'=4,'ref'=8] {'ref'}, use_global_device_ids=true, to_apply=%region_5.6 | all-reduce | flops 16 | bytes 128 | tf_op jit(solution)/shard_map/pmax | solution.py:70
  103.0 0.1 fusion.53
  103.2 15.3 %all-reduce = (f32[16]{0:T(128)S(1)}, f32[16,4]{0,1:T(4,128)S(1)}) all-reduce(f32[16]{0:T(128)S(1)} %fusion.51, f32[16,4]{0,1:T(4,128)S(1)} %fusion.53), channel_id=1, replica_groups=mesh['img'=4,'ref'=8] {'ref'}, use_global_device_ids=true, to_apply=%region_7.8 | all-reduce | flops 80 | bytes 640 | tf_op jit(solution)/shard_map/psum | solution.py:75
  118.5 25.5 %while.22 = (s32[]{:T(128)}, f32[2,8,32768]{2,1,0:T(8,128)S(1)}, bf16[3,16,32]{1,2,0:T(8,128)(2,1)S(1)}, bf16[2,16,32768]{2,1,0:T(8,128)(2,1)}, f32[3,4,32768]{2...) while((s32[]{:T(128)}, f32[2,8,32768]{2,1,0:T(8,128)S(1)}, ...), condition=%wide.region_11.12_spmd.clone, body=%wide.region_8.11_spmd.clone.sunk | while | flops 76546048 | bytes 30425728 | solution.py:91
  118.5 1.9 fusion.73
  120.5 1.4 dynamic-slice_bitcast_fusion.7
  121.9 0.5 copy-done.2
  122.4 2.9 %subtract_reduce_fusion.2 = (f32[8,32768]{1,0:T(8,128)S(1)}, f32[8,32768]{1,0:T(8,128)}) fusion(f32[4,8,32768]{2,1,0:T(8,128)S(1)} %fusion.73, f32[4,32768]{1,0:T(4,128)S(1)} %get-tuple-element.215, f32[4,32768]{1,0:T(4,128)S(1)} %get-tuple-element.216, bf16[2,16,32768]{2,1,0:T(8,128)(2,1)S(1)} %copy-done.2, ...), kind=kOutput, calls=%fused_computation.26.clone.1 | convolution fusion | flops 41418752 | bytes 8396804 | tf_op jit(solution)/shard_map/while/body/eval_jaxpr/dot_general | solution.py:31
  125.2 1.8 maximum_add_fusion.2
  127.1 1.9 fusion.73
  129.0 1.4 dynamic-slice_bitcast_fusion.7
  130.4 0.5 copy-done.2
  130.9 2.9 %subtract_reduce_fusion.2 = (f32[8,32768]{1,0:T(8,128)S(1)}, f32[8,32768]{1,0:T(8,128)}) fusion(f32[4,8,32768]{2,1,0:T(8,128)S(1)} %fusion.73, f32[4,32768]{1,0:T(4,128)S(1)} %get-tuple-element.215, f32[4,32768]{1,0:T(4,128)S(1)} %get-tuple-element.216, bf16[2,16,32768]{2,1,0:T(8,128)(2,1)S(1)} %copy-done.2, ...), kind=kOutput, calls=%fused_computation.26.clone.1 | convolution fusion | flops 41418752 | bytes 8396804 | tf_op jit(solution)/shard_map/while/body/eval_jaxpr/dot_general | solution.py:31
  133.7 1.8 maximum_add_fusion.2
  135.6 1.9 fusion.73
  137.5 1.4 dynamic-slice_bitcast_fusion.7
  138.9 0.5 copy-done.2
  139.4 2.9 %subtract_reduce_fusion.2 = (f32[8,32768]{1,0:T(8,128)S(1)}, f32[8,32768]{1,0:T(8,128)}) fusion(f32[4,8,32768]{2,1,0:T(8,128)S(1)} %fusion.73, f32[4,32768]{1,0:T(4,128)S(1)} %get-tuple-element.215, f32[4,32768]{1,0:T(4,128)S(1)} %get-tuple-element.216, bf16[2,16,32768]{2,1,0:T(8,128)(2,1)S(1)} %copy-done.2, ...), kind=kOutput, calls=%fused_computation.26.clone.1 | convolution fusion | flops 41418752 | bytes 8396804 | tf_op jit(solution)/shard_map/while/body/eval_jaxpr/dot_general | solution.py:31
  142.3 1.8 maximum_add_fusion.2
  144.1 1.3 copy-done
  145.5 0.2 divide_reduce_fusion
  145.7 13.0 %psum.22 = f32[8]{0:T(128)S(1)} all-reduce(f32[8]{0:T(128)S(1)} %reduce_sum.75), channel_id=1, replica_groups=mesh['img'=4,'ref'=8] {'img'}, use_global_device_ids=true, to_apply=%region_15.16 | all-reduce | flops 8 | bytes 64 | tf_op jit(solution)/shard_map/psum | solution.py:93
  158.7 0.6 broadcast_divide_fusion.1
  159.3 26.8 %reduce-scatter.2.cloned.1.call-done = f32[2,8,8192]{2,1,0:T(8,128)} async-done(((f32[2,8,32768]{2,1,0:T(8,128)}), f32[2,8,8192]{2,1,0:T(8,128)}) %reduce-scatter.2.cloned.1.call-update) | async-done | bytes 524304 | tf_op jit(solution)/shard_map/reduce_scatter | solution.py:92
  186.1 1.9 broadcast_divide_fusion
  (41 shorter events, 1.3 us)
Async XLA Ops:
  7.2 3.8 %copy-start.4 = (s32[12,2]{0,1:T(2,128)S(1)}, s32[12,2]{0,1:T(2,128)}, u32[]{:S(2)}) copy-start(s32[12,2]{0,1:T(2,128)} %param.13) | copy-start | bytes 292
  7.2 21.1 %all-gather.3.cloned.1.call-start = ((), (), s32[]{:S(2)}) async-start(), calls=%async_computation.1 | async-start | bytes 1310720 | tf_op jit(solution)/shard_map/all_gather | solution.py:38
  9.0 68.8 %all-gather.5.cloned.1.call-start = ((), (), s32[]{:S(2)}) async-start(), calls=%async_computation.2 | async-start | bytes 2359296 | tf_op jit(solution)/shard_map/all_gather | solution.py:37
  10.8 12.9 %copy-start.5 = (s32[8]{0:T(128)S(1)}, s32[8]{0:T(128)}, u32[]{:S(2)}) copy-start(s32[8]{0:T(128)} %param.14) | copy-start | bytes 100
  10.8 12.9 %copy-start.6 = (f32[4]{0:T(128)S(1)}, f32[4]{0:T(128)}, u32[]{:S(2)}) copy-start(f32[4]{0:T(128)} %param.15) | copy-start | bytes 52
  10.9 175.2 %reduce-scatter.2.cloned.1.call-start = ((), (), s32[]{:S(2)}) async-start(), calls=%async_computation.3 | async-start | bytes 2621440 | tf_op jit(solution)/shard_map/reduce_scatter | solution.py:92
  77.8 12.8 %copy-start.3 = (f32[16]{0:T(128)S(1)}, f32[16]{0:T(128)}, u32[]{:S(2)}) copy-start(f32[16]{0:T(128)} %param.12) | copy-start | bytes 196
  79.1 1.6 copy-start.1
  83.4 1.6 copy-start.1
  87.6 1.6 copy-start.1
  120.4 1.9 copy-start.2
  129.0 1.9 copy-start.2
  137.5 1.9 copy-start.2
  144.1 1.4 copy-start
Sparse Core Ops, SparseCore 0:
  10.1 18.0 all-gather.2
  30.5 47.3 all-gather.4
  145.6 40.4 reduce-scatter.1
where the time goes:
time: 197 us; the launch traced here: 195 us
  waiting for transfers between devices  77.4 us (39%)
  blocking collectives  40.3 us (20%)
  other arithmetic  28.1 us (14%)
  matrix products  18.5 us (9%)
  local copies, waits for them, and re-layouts  16.1 us (8%)
  between operations  13.8 us (7%)
    all_gather x1, waiting for transfers between devices, local(): lax.all_gather(images.astype(jnp.bfloat16), 'ref', axis=2, tiled=True)  46.2 us
    reduce_scatter x1, waiting for transfers between devices, local(): lax.psum_scatter(summed, 'img', scatter_dimension=2, tiled=True)  26.8 us
    psum x1, blocking collectives, local(): lax.psum((jnp.sum(exponent, axis=(1, 2)), local_class), 'ref')  15.3 us
    dot_general x6, matrix products, inner_cols(): lax.dot_general(left, right, (((0,), (0,)), ((), ())), preferred_element_...  14.3 us
    psum x1, blocking collectives, local(): ref_mass = lax.psum(local_mass, 'img')  13 us
    sin x1, other arithmetic, phases(): return (jnp.cos(angles), jnp.sin(angles))  12.6 us
    pmax x1, blocking collectives, local(): top_score = lax.pmax(local_top, 'ref')  12.1 us
    while x12, local copies, waits for them, and re-layouts  5.74 us
  transfers between devices with their start and end apart: 3, of which 3 were waited for; matrix products, arithmetic and copies ran while one was open for 10% of the time, Pallas kernels for 0%

commit v1 on v0

--- a/solution.py
+++ b/solution.py
@@ -1,8 +1,11 @@
+import functools
 import math
 
 import jax
 import jax.numpy as jnp
 from jax import lax
+from jax.experimental import pallas as pl
+from jax.experimental.pallas import tpu as pltpu
 from jax.sharding import PartitionSpec as P
 
 ROWS = 256
@@ -33,7 +36,7 @@
     )
 
 
-def local(images, references, precision, shifts, labels, log_prior):
+def gathered(images, references, precision, shifts, labels, log_prior):
     img_low = lax.all_gather(images.astype(jnp.bfloat16), "ref", axis=2, tiled=True)
     ref_low = lax.all_gather(references.astype(jnp.bfloat16), "img", axis=2, tiled=True)
     pixels = img_low.shape[2]
@@ -95,9 +98,378 @@
     return (new_refs, class_post)
 
 
+MESH = pl.DeviceIdType.MESH
+LANES = 128
+CHUNK = 1024
+OWNED = 2
+PAIRS = SHIFTS // 2
+REF_ROWS = 8
+
+
+def exchange(src, dst, send_sem, recv_sem, img, ref):
+    return pltpu.make_async_remote_copy(
+        src_ref=src, dst_ref=dst, send_sem=send_sem, recv_sem=recv_sem, device_id=(img, ref), device_id_type=MESH
+    )
+
+
+def fused_kernel(
+    n_img, n_ref,
+    images, references, precision, shifts, labels, log_prior,
+    new_refs, class_post,
+    img_send, img_buf, ref_send, ref_buf, cos_tab, sin_tab, rotated, shifted,
+    part, part_in, own, own_in, post_buf, post_wide, out_send, out_buf,
+    img_ss, img_rs, ref_ss, ref_rs, part_ss, part_rs, own_ss, own_rs, post_ss, post_rs, out_ss, out_rs,
+):
+    n_dev = n_img * n_ref
+    a = lax.axis_index("img")
+    r = lax.axis_index("ref")
+    me = a * n_ref + r
+    per = n_ref // n_img
+    img_dev = images.shape[1]
+    n_images = n_img * img_dev
+    n_refs = n_ref * REF_ROWS
+
+    barrier = pltpu.get_barrier_semaphore()
+
+    def greet(j, carry):
+        other = lax.rem(me + j, n_dev)
+        pl.semaphore_signal(barrier, inc=1, device_id=(other // n_ref, lax.rem(other, n_ref)), device_id_type=MESH)
+        return carry
+
+    lax.fori_loop(1, n_dev, greet, 0)
+
+    for q in range(n_ref):
+        px = pl.ds(q * CHUNK, CHUNK)
+        both = jnp.concatenate([references[0, :, px], references[1, :, px]], axis=0)
+        ref_send[q, :, 0:CHUNK] = both.astype(jnp.bfloat16)
+    label_col = jnp.broadcast_to(labels[...].astype(jnp.float32), (REF_ROWS, LANES))
+    label_block = jnp.concatenate([label_col, label_col], axis=0).astype(jnp.bfloat16)
+    for q in range(n_ref):
+        ref_send[q, :, CHUNK : CHUNK + LANES] = label_block
+    for q in range(n_img):
+        img_send[q] = images[:, :, q * CHUNK : (q + 1) * CHUNK].astype(jnp.bfloat16)
+    img_buf[a] = img_send[a]
+
+    pl.semaphore_wait(barrier, n_dev - 1)
+
+    def ref_copy(q):
+        return exchange(
+            ref_send.at[q], ref_buf.at[r], ref_ss.at[q], ref_rs.at[r], lax.rem(q, n_img), per * a + q // n_img
+        )
+
+    def ref_here(q):
+        return (lax.rem(q, n_img) == a) & (per * a + q // n_img == r)
+
+    def ref_start(j, carry):
+        q = lax.rem(me + j, n_ref)
+
+        @pl.when(ref_here(q))
+        def _():
+            ref_buf[r] = ref_send[q]
+
+        @pl.when(jnp.logical_not(ref_here(q)))
+        def _():
+            ref_copy(q).start()
+
+        return carry
+
+    lax.fori_loop(0, n_ref, ref_start, 0)
+
+    img_copies = []
+    for j in range(1, n_img):
+        dest = lax.rem(a + j, n_img)
+        copy = exchange(img_send.at[dest], img_buf.at[a], img_ss.at[j], img_rs.at[j], dest, r)
+        copy.start()
+        img_copies.append(copy)
+
+    row_first = r * (n_img * CHUNK // COLS) + a * (CHUNK // COLS) - ROWS // 2
+    freq_y = lax.broadcasted_iota(jnp.int32, (CHUNK // COLS, COLS), 0) + row_first
+    freq_x = lax.broadcasted_iota(jnp.int32, (CHUNK // COLS, COLS), 1)
+
+    def phase_row(t, carry):
+        turn = freq_x * shifts[t, 0] + freq_y * shifts[t, 1]
+        turn = ((turn + ROWS // 2) & (ROWS - 1)) - ROWS // 2
+        angle = turn.astype(jnp.float32) * (2.0 * math.pi / ROWS)
+        cosine = jnp.cos(angle)
+        sine = jnp.sin(angle)
+        for y in range(CHUNK // COLS):
+            cos_tab[t, :, y * COLS : (y + 1) * COLS] = jnp.broadcast_to(cosine[y : y + 1], (8, COLS))
+            sin_tab[t, :, y * COLS : (y + 1) * COLS] = jnp.broadcast_to(sine[y : y + 1], (8, COLS))
+        return carry
+
+    lax.fori_loop(0, SHIFTS, phase_row, 0)
+
+    for copy in img_copies:
+        copy.wait_recv()
+
+    def rotate(t, carry):
+        cos_row = cos_tab[t][None]
+        sin_row = sin_tab[t][None]
+        for b in range(n_img):
+            re = img_buf[b, 0].astype(jnp.float32).reshape(img_dev // 8, 8, CHUNK)
+            im = img_buf[b, 1].astype(jnp.float32).reshape(img_dev // 8, 8, CHUNK)
+            rows = pl.ds(b * img_dev, img_dev)
+            turned_re = (re * cos_row - im * sin_row).reshape(img_dev, CHUNK)
+            turned_im = (im * cos_row + re * sin_row).reshape(img_dev, CHUNK)
+            rotated[t, rows, 0:CHUNK] = turned_re.astype(jnp.bfloat16)
+            rotated[t, rows, CHUNK : 2 * CHUNK] = turned_im.astype(jnp.bfloat16)
+        return carry
+
+    lax.fori_loop(0, SHIFTS, rotate, 0)
+
+    def ref_arrive(j, carry):
+        @pl.when(jnp.logical_not((a == r // per) & (j == r)))
+        def _():
+            exchange(ref_send.at[0], ref_buf.at[j], ref_ss.at[0], ref_rs.at[j], r // per, j).wait_recv()
+
+        return carry
+
+    lax.fori_loop(0, n_ref, ref_arrive, 0)
+
+    def shift(t, carry):
+        cos_row = cos_tab[t]
+        sin_row = sin_tab[t]
+        for b in range(0, n_ref, 2):
+            res = []
+            ims = []
+            for s in range(2):
+                block = ref_buf[b + s, :, 0:CHUNK].astype(jnp.float32)
+                re = block[0:REF_ROWS]
+                im = block[REF_ROWS : 2 * REF_ROWS]
+                res.append(re * cos_row + im * sin_row)
+                ims.append(im * cos_row - re * sin_row)
+            rows = pl.ds(b * REF_ROWS, 2 * REF_ROWS)
+            shifted[t, rows, 0:CHUNK] = jnp.concatenate(res, axis=0).astype(jnp.bfloat16)
+            shifted[t, rows, CHUNK : 2 * CHUNK] = jnp.concatenate(ims, axis=0).astype(jnp.bfloat16)
+        return carry
+
+    lax.fori_loop(0, SHIFTS, shift, 0)
+
+    energies = []
+    label_rows = []
+    for b in range(n_ref):
+        block = ref_buf[b, :, 0:CHUNK].astype(jnp.float32)
+        square = jnp.sum(block * block, axis=1, keepdims=True)
+        energies.append(square[0:REF_ROWS] + square[REF_ROWS : 2 * REF_ROWS])
+        label_rows.append(ref_buf[b, :, CHUNK : CHUNK + LANES].astype(jnp.float32)[0:REF_ROWS])
+    energy = jnp.broadcast_to(jnp.concatenate(energies + energies, axis=0), (2 * n_refs, LANES)).T
+    half_energy = 0.5 * energy[0:8][None]
+    label_lane = jnp.concatenate(label_rows + label_rows, axis=0).T[0:8]
+
+    pictures = [img_buf[:, c].reshape(n_images, CHUNK) for c in range(2)]
+    pictures = jnp.concatenate(pictures, axis=1)
+    for tp in range(PAIRS):
+        pair = shifted[2 * tp : 2 * tp + 2].reshape(2 * n_refs, 2 * CHUNK)
+        cross = inner_rows(pictures, pair)
+        cross = (cross.reshape(n_images // 8, 8, LANES) - half_energy).reshape(n_img, img_dev, LANES)
+        part[:, :, tp * LANES : (tp + 1) * LANES] = cross
+
+    part_copies = []
+    for j in range(1, n_img):
+        dest = lax.rem(a + j, n_img)
+        copy = exchange(part.at[dest], part_in.at[j - 1], part_ss.at[j], part_rs.at[j], dest, r)
+        copy.start()
+        part_copies.append(copy)
+    own[...] = jnp.zeros_like(own)
+    for copy in part_copies:
+        copy.wait_recv()
+    total = part[a]
+    for j in range(n_img - 1):
+        total = total + part_in[j]
+    for tp in range(PAIRS):
+        own[:, tp, :] = total[:, tp * LANES : (tp + 1) * LANES]
+    own_copies = []
+    for j in range(1, n_ref):
+        dest = lax.rem(r + j, n_ref)
+        copy = exchange(own.at[pl.ds(OWNED * dest, OWNED)], own_in.at[j - 1], own_ss.at[j], own_rs.at[j], a, dest)
+        copy.start()
+        own_copies.append(copy)
+    prior = jnp.zeros((8, LANES), jnp.float32)
+    for c in range(CLASSES):
+        prior = prior + jnp.where(label_lane == c, log_prior[c], 0.0)
+    for copy in own_copies:
+        copy.wait_recv()
+    mine = own[pl.ds(OWNED * r, OWNED)]
+    for j in range(n_ref - 1):
+        mine = mine + own_in[j]
+
+    row = lax.broadcasted_iota(jnp.int32, (8, LANES), 0)
+    lane = lax.broadcasted_iota(jnp.int32, (8, LANES), 1)
+    blocks = []
+    for il in range(OWNED):
+        scores = precision[OWNED * r + il] * mine[il] + prior
+        scores = jnp.where(row < PAIRS, scores, -jnp.inf)
+        top = jnp.max(jnp.max(scores, axis=1, keepdims=True), axis=0, keepdims=True)
+        exponent = jnp.exp(scores - top)
+        row_total = jnp.sum(jnp.sum(exponent, axis=1, keepdims=True), axis=0, keepdims=True)
+        posterior = exponent / row_total
+        lane_sum = jnp.broadcast_to(jnp.sum(posterior, axis=0, keepdims=True), (8, LANES))
+        totals = lane_sum + pltpu.roll(lane_sum, n_refs, 1)
+        for c in range(CLASSES):
+            in_class = jnp.sum(jnp.where(label_lane == c, lane_sum, 0.0), axis=1, keepdims=True)
+            totals = jnp.where(lane == n_refs + c, in_class, totals)
+        high = totals.astype(jnp.bfloat16).astype(jnp.float32)
+        block = jnp.where(row == PAIRS, high, posterior)
+        blocks.append(jnp.where(row == PAIRS + 1, totals - high, block))
+    post_buf[me] = jnp.concatenate(blocks, axis=0).astype(jnp.bfloat16)
+
+    def post_copy(j):
+        other = lax.rem(me + j, n_dev)
+        return exchange(
+            post_buf.at[me], post_buf.at[me], post_ss.at[j], post_rs.at[j], other // n_ref, lax.rem(other, n_ref)
+        )
+
+    def post_start(j, carry):
+        post_copy(j).start()
+        return carry
+
+    lax.fori_loop(1, n_dev, post_start, 0)
+
+    def post_arrive(j, carry):
+        source = lax.rem(me + n_dev - j, n_dev)
+        exchange(
+            post_buf.at[me], post_buf.at[source], post_ss.at[j], post_rs.at[j], source // n_ref, lax.rem(source, n_ref)
+        ).wait_recv()
+        return carry
+
+    lax.fori_loop(1, n_dev, post_arrive, 0)
+
+    post_wide[...] = post_buf[...].astype(jnp.float32).reshape(n_images, 8, LANES)
+    totals = post_wide[:, PAIRS, :] + post_wide[:, PAIRS + 1, :]
+    mass = jnp.broadcast_to(jnp.sum(totals, axis=0, keepdims=True), (LANES, LANES)).T[0:n_refs]
+    scale = 1.0 / (mass[:, 0:1] + 1.0)
+    first = pl.ds(a * img_dev, img_dev)
+    class_post[...] = post_wide[first, PAIRS, :] + post_wide[first, PAIRS + 1, :]
+    weights = []
+    for tp in range(PAIRS):
+        both = post_wide[:, tp, :].T
+        weights.append(jnp.concatenate([both[0:n_refs], both[n_refs : 2 * n_refs]], axis=1).astype(jnp.bfloat16))
+    weights = jnp.concatenate(weights, axis=1)
+    turned = rotated[...].reshape(SHIFTS * n_images, 2 * CHUNK)
+    summed = jnp.dot(weights, turned, preferred_element_type=jnp.float32) * scale
+    low = summed.reshape(n_ref, REF_ROWS, 2 * CHUNK)
+    for b in range(n_ref):
+        both = jnp.concatenate([low[b, :, 0:CHUNK], low[b, :, CHUNK : 2 * CHUNK]], axis=0)
+        out_send[b] = both.astype(jnp.bfloat16)
+
+    piece = lax.rem(r, per) * n_img + a
+
+    def out_copy(j):
+        return exchange(out_send.at[j], out_buf.at[piece], out_ss.at[j], out_rs.at[piece], r // per, j)
+
+    def out_start(i, carry):
+        j = lax.rem(r + i, n_ref)
+        here = (a == r // per) & (j == r)
+
+        @pl.when(here)
+        def _():
+            out_buf[piece] = out_send[j]
+
+        @pl.when(jnp.logical_not(here))
+        def _():
+            out_copy(j).start()
+
+        return carry
+
+    lax.fori_loop(0, n_ref, out_start, 0)
+
+    for q in range(n_ref):
+        @pl.when(jnp.logical_not(ref_here(q)))
+        def _():
+            exchange(
+                out_send.at[0], out_buf.at[q], out_ss.at[0], out_rs.at[q], q % n_img, per * a + q // n_img
+            ).wait_recv()
+
+        block = out_buf[q].astype(jnp.float32)
+        new_refs[0, :, q * CHUNK : (q + 1) * CHUNK] = block[0:REF_ROWS]
+        new_refs[1, :, q * CHUNK : (q + 1) * CHUNK] = block[REF_ROWS : 2 * REF_ROWS]
+
+    for copy in img_copies + part_copies + own_copies:
+        copy.wait_send()
+
+    def post_sent(j, carry):
+        post_copy(j).wait_send()
+        return carry
+
+    lax.fori_loop(1, n_dev, post_sent, 0)
+
+    def edge_sent(j, carry):
+        @pl.when(jnp.logical_not(ref_here(j)))
+        def _():
+            ref_copy(j).wait_send()
+
+        @pl.when(jnp.logical_not((a == r // per) & (j == r)))
+        def _():
+            out_copy(j).wait_send()
+
+        return carry
+
+    lax.fori_loop(0, n_ref, edge_sent, 0)
+
+
+def fused(n_img, n_ref, images, references, precision, shifts, labels, log_prior):
+    img_dev = images.shape[1]
+    n_images = n_img * img_dev
+    n_refs = n_ref * REF_ROWS
+    n_dev = n_img * n_ref
+    vmem = pl.BlockSpec(memory_space=pltpu.VMEM)
+    smem = pl.BlockSpec(memory_space=pltpu.SMEM)
+    low = jnp.bfloat16
+    wide = jnp.float32
+    counts = (n_img, n_img, n_ref, n_ref, n_img, n_img, n_ref, n_ref, n_dev, n_dev, n_ref, n_ref)
+    new_refs, class_rows = pl.pallas_call(
+        functools.partial(fused_kernel, n_img, n_ref),
+        out_shape=(
+            jax.ShapeDtypeStruct(references.shape, wide),
+            jax.ShapeDtypeStruct((img_dev, LANES), wide),
+        ),
+        in_specs=[vmem, vmem, smem, smem, vmem, smem],
+        out_specs=(vmem, vmem),
+        scratch_shapes=[
+            pltpu.VMEM((n_img, 2, img_dev, CHUNK), low),
+            pltpu.VMEM((n_img, 2, img_dev, CHUNK), low),
+            pltpu.VMEM((n_ref, 2 * REF_ROWS, CHUNK + LANES), low),
+            pltpu.VMEM((n_ref, 2 * REF_ROWS, CHUNK + LANES), low),
+            pltpu.VMEM((SHIFTS, 8, CHUNK), wide),
+            pltpu.VMEM((SHIFTS, 8, CHUNK), wide),
+            pltpu.VMEM((SHIFTS, n_images, 2 * CHUNK), low),
+            pltpu.VMEM((SHIFTS, n_refs, 2 * CHUNK), low),
+            pltpu.VMEM((n_img, img_dev, PAIRS * LANES), wide),
+            pltpu.VMEM((n_img - 1, img_dev, PAIRS * LANES), wide),
+            pltpu.VMEM((img_dev, 8, LANES), wide),
+            pltpu.VMEM((n_ref - 1, OWNED, 8, LANES), wide),
+            pltpu.VMEM((n_dev, 16, LANES), low),
+            pltpu.VMEM((n_images, 8, LANES), wide),
+            pltpu.VMEM((n_ref, 2 * REF_ROWS, CHUNK), low),
+            pltpu.VMEM((n_ref, 2 * REF_ROWS, CHUNK), low),
+        ]
+        + [pltpu.SemaphoreType.DMA((count,)) for count in counts],
+        compiler_params=pltpu.CompilerParams(
+            collective_id=0, has_side_effects=True, vmem_limit_bytes=40 * 1024 * 1024
+        ),
+        cost_estimate=pl.CostEstimate(flops=800_000_000, bytes_accessed=2_000_000, transcendentals=25_000),
+    )(images, references, precision, shifts, labels.reshape(REF_ROWS, 1), log_prior)
+    return new_refs, class_rows[:, n_refs : n_refs + CLASSES]
+
+
+def local(n_img, n_ref, images, references, precision, shifts, labels, log_prior):
+    fits = (
+        images.shape[1] == OWNED * n_ref
+        and images.shape[1] % 16 == 0
+        and references.shape[1] == REF_ROWS
+        and 2 * n_ref * REF_ROWS == LANES
+        and images.shape[2] == n_img * CHUNK
+        and references.shape[2] == n_ref * CHUNK
+        and n_ref % n_img == 0
+    )
+    if fits:
+        return fused(n_img, n_ref, images, references, precision, shifts, labels, log_prior)
+    return gathered(images, references, precision, shifts, labels, log_prior)
+
+
 def solution(mesh):
     return jax.shard_map(
-        local,
+        functools.partial(local, mesh.shape["img"], mesh.shape["ref"]),
         mesh=mesh,
         in_specs=(P(None, "img", "ref"), P(None, "ref", "img"), P("img"), P(), P("ref"), P()),
         out_specs=(P(None, "ref", "img"), P("img", None)),

time: 197 us -> 52.1 us (0.26)
  waiting for transfers between devices: 77.4 us -> 0 us
  Pallas kernels: 0 us -> 45.3 us
  blocking collectives: 40.3 us -> 0 us
  other arithmetic: 28.1 us -> 0 us
  matrix products: 18.5 us -> 0 us
  between operations: 13.8 us -> 0.65 us
  local copies, waits for them, and re-layouts: 16.1 us -> 5.6 us
    all_gather x2 -> x0, waiting for transfers between devices: 50.5 us -> none  [the longest x1 46.2 us: local(): lax.all_gather(images.astype(jnp.bfloat16), 'ref', axis=2, tiled=True)]
    pallas_call x0 -> x1, Pallas kernels: none -> 45.3 us  [fused(): pl.pallas_call(functools.partial(fused_kernel, n_img, n_ref), out_shape=(...]
    psum x2 -> x0, blocking collectives: 28.2 us -> none  [the longest x1 15.3 us: local(): lax.psum((jnp.sum(exponent, axis=(1, 2)), local_class), 'ref')]
    reduce_scatter x1 -> x0, waiting for transfers between devices: 26.8 us -> none  [local(): lax.psum_scatter(summed, 'img', scatter_dimension=2, tiled=True)]
    dot_general x13 -> x0, matrix products: 18.5 us -> none  [the longest x6 14.3 us: inner_cols(): lax.dot_general(left, right, (((0,), (0,)), ((), ())), preferred_element_...]
    sin x1 -> x0, other arithmetic: 12.6 us -> none  [phases(): return (jnp.cos(angles), jnp.sin(angles))]
    pmax x1 -> x0, blocking collectives: 12.1 us -> none  [local(): top_score = lax.pmax(local_top, 'ref')]
    mul x11 -> x0, local copies, waits for them, and re-layouts: 8.67 us -> none  [the longest x3 4.27 us: back_block(): back_im * sin_rows[:, None, :]]
  transfers between devices with their start and end apart: 3 -> 0, of which waited for: 3 -> 0; matrix products, arithmetic and copies ran while one was open for 10% -> 0% of each run, Pallas kernels for 0% -> 0%
where the time goes in v1:
time: 52.1 us; the launch traced here: 51.5 us
  Pallas kernels  45.3 us (87%)
  local copies, waits for them, and re-layouts  5.6 us (11%)
  between operations  0.65 us (1%)
    pallas_call x1, Pallas kernels, fused(): pl.pallas_call(functools.partial(fused_kernel, n_img, n_ref), out_shape=(...  45.3 us
    unnamed x15, local copies, waits for them, and re-layouts  5.45 us

profile of v1, /device:TPU:25, one launch (start us, length us, event | category | flops | bytes accessed | tf_op | source)
XLA Modules:
  0.0 51.5 jit_solution(8926395798642859746)
XLA Ops:
  0.6 0.0 copy-start.5
  0.6 0.6 %copy-done.5 = s32[8]{0:T(128)S(1)} copy-done((s32[8]{0:T(128)S(1)}, s32[8]{0:T(128)}, u32[]{:S(2)}) %copy-start.5) | copy-done | bytes 56
  1.3 0.0 copy-start.4
  1.3 0.1 copy.9.labels
  1.4 0.6 %copy-done.4 = s32[12,2]{0,1:T(2,128)S(1)} copy-done((s32[12,2]{0,1:T(2,128)S(1)}, s32[12,2]{0,1:T(2,128)}, u32[]{:S(2)}) %copy-start.4) | copy-done | bytes 120
  2.0 0.0 copy-start.2
  2.0 0.0 copy-start.3
  2.0 0.1 copy.8.shifts
  2.1 0.6 %copy-done.2 = f32[16]{0:T(128)S(1)} copy-done((f32[16]{0:T(128)S(1)}, f32[16]{0:T(128)}, u32[]{:S(2)}) %copy-start.2) | copy-done | bytes 88
  2.6 0.0 copy-done.3
  2.6 0.0 copy-start
  2.6 1.0 %copy-done = f32[2,16,4096]{2,1,0:T(8,128)S(1)} copy-done((f32[2,16,4096]{2,1,0:T(8,128)S(1)}, f32[2,16,4096]{2,1,0:T(8,128)}, u32[]{:S(2)}) %copy-start) | copy-done | bytes 524312
  3.7 0.0 copy-start.1
  3.7 1.0 %copy-done.1 = f32[2,8,8192]{2,1,0:T(8,128)S(1)} copy-done((f32[2,8,8192]{2,1,0:T(8,128)S(1)}, f32[2,8,8192]{2,1,0:T(8,128)}, u32[]{:S(2)}) %copy-start.1) | copy-done | bytes 524312
  4.7 45.3 %shard_map.77 = (f32[2,8,8192]{2,1,0:T(8,128)S(1)}, f32[16,128]{1,0:T(8,128)S(1)}) custom-call(f32[2,16,4096]{2,1,0:T(8,128)S(1)} %copy-done, f32[2,8,8192]{2,1,0:T(8,128)S(1)} %copy-done.1, f32[16]{0:T(128)S(1)} %copy-done.2, s32[12,2]{1,0:T(8,128)S(1)} %copy.8.shifts, s32[8,1]{1,0:T(8,128)S(1)} %copy.9.labels, f32[4]{0:T(128)S(1)} %copy-done.3), custom_call_target="tpu_custom_call" | custom-call | flops 800000000 | bytes 2000000 | tf_op jit(solution)/shard_map/pallas_call | solution.py:420
  50.0 0.1 slice.3
  50.1 0.7 %copy.10 = f32[16,4]{0,1:T(4,128)} copy(f32[16,4]{1,0:T(8,128)S(1)} %slice.3) | data formatting | bytes 512
  50.7 0.8 %copy.12 = f32[2,8,8192]{2,1,0:T(8,128)} copy(f32[2,8,8192]{2,1,0:T(8,128)S(1)} %get-tuple-element.10) | data formatting | bytes 1048576
Async XLA Ops:
  0.6 0.7 %copy-start.5 = (s32[8]{0:T(128)S(1)}, s32[8]{0:T(128)}, u32[]{:S(2)}) copy-start(s32[8]{0:T(128)} %param.10) | copy-start | bytes 100
  1.3 0.7 %copy-start.4 = (s32[12,2]{0,1:T(2,128)S(1)}, s32[12,2]{0,1:T(2,128)}, u32[]{:S(2)}) copy-start(s32[12,2]{0,1:T(2,128)} %param.9) | copy-start | bytes 292
  2.0 0.7 %copy-start.2 = (f32[16]{0:T(128)S(1)}, f32[16]{0:T(128)}, u32[]{:S(2)}) copy-start(f32[16]{0:T(128)} %precision.1) | copy-start | bytes 196
  2.0 0.7 %copy-start.3 = (f32[4]{0:T(128)S(1)}, f32[4]{0:T(128)}, u32[]{:S(2)}) copy-start(f32[4]{0:T(128)} %log_prior.1) | copy-start | bytes 52
  2.6 1.0 %copy-start = (f32[2,16,4096]{2,1,0:T(8,128)S(1)}, f32[2,16,4096]{2,1,0:T(8,128)}, u32[]{:S(2)}) copy-start(f32[2,16,4096]{2,1,0:T(8,128)} %images.1) | copy-start | bytes 1572868
  3.7 1.0 %copy-start.1 = (f32[2,8,8192]{2,1,0:T(8,128)S(1)}, f32[2,8,8192]{2,1,0:T(8,128)}, u32[]{:S(2)}) copy-start(f32[2,8,8192]{2,1,0:T(8,128)} %references.1) | copy-start | bytes 1572868
